TPU v7x, 1024 devices: a whole 8x8x8 slice. The times are simulated.
1024 devices in a mesh: ctx: 16 (over x_lo, y), exp: 64 (over x_hi, z, core).
Axes of the slice: x: 8 (x_hi: 4, x_lo: 2; x = x_hi * 2 + x_lo), y: 8, z: 8, core: 2. Of those that a mesh axis runs over, the one named last changes fastest.
Arguments:
- queries: bfloat16 [2048, 36864], P('ctx', 'exp'), may hold values from -400 to 400
- latents: bfloat16 [2048, 576], P('ctx'), may hold values from -6 to 6
- group_order: int32 [64], replicated, may hold values from 0 to 63, each once
- hidden_b: bfloat16 [512, 7168], P('exp', 'ctx'), may hold values from -6 to 6
- expert_ids: int32 [512, 8], P('exp'), may hold values from 0 to 63, all different within a row; in each aligned block of 8 rows (0 to 7, 8 to 15, ...) at most 2 rows name the same one
- gate_fixed: int32 [512, 8], P('exp'), may hold values from 4096 to 32767
- w_gate: bfloat16 [64, 7168, 1024], P('exp', 'ctx'), may hold values from -0.0625 to 0.0625
- w_up: bfloat16 [64, 7168, 1024], P('exp', 'ctx'), may hold values from -0.0625 to 0.0625
- w_down: bfloat16 [64, 1024, 7168], P('exp', None, 'ctx'), may hold values from -0.1875 to 0.1875
Outputs:
- attn_out: bfloat16 [2048, 32768], P('ctx', 'exp')
- moe_out: bfloat16 [512, 7168], P('exp', 'ctx')
Inputs may be any that keep to these rules, and one draw needn't show every extreme that they name: `group_order`: each block position appears once. `expert_ids`: each row names 8 different experts. Within the 8 rows of one index of exp (aligned blocks of 8 rows) no expert is named more than 2 times, a bound that some block reaches.
All inputs are finite; a program needn't handle non-finite values.
Results may differ from a plain program's by a relative error of at most 0.006.
Values may be sent and summed in bfloat16 or wider, within the bound.
A program may use at most 32 MiB of HBM per device.

v0:
```python
import math

import jax
import jax.numpy as jnp
from jax import lax
from jax.sharding import PartitionSpec as P

KV_RANK = 512
SUB = 4


SCALE = 1.0 / math.sqrt(192.0)


def prompt_positions(group_order, row_index, block_rows):
    owner = row_index // block_rows
    group_ids = jnp.arange(group_order.shape[0], dtype=jnp.int32)
    matches = (owner[:, None] == group_ids[None, :]).astype(jnp.int32)
    return jnp.sum(matches * group_order[None, :], axis=1) * block_rows + row_index % block_rows


def attend_head(q_head, keys, query_pos, key_pos):
    scores = (
        lax.dot_general(q_head, keys, (((1,), (1,)), ((), ())), preferred_element_type=jnp.float32)
        * SCALE
    )
    scores = jnp.where(key_pos[None, :] <= query_pos[:, None], scores, jnp.float32(-1e30))
    top_score = jnp.max(scores, axis=1, keepdims=True)
    raised = jnp.exp(scores - top_score)
    probs = (raised / jnp.sum(raised, axis=1, keepdims=True)).astype(jnp.bfloat16)
    return jnp.dot(probs, keys[:, :KV_RANK], preferred_element_type=jnp.float32).astype(
        jnp.bfloat16
    )


def attention_part(queries, latents, group_order):
    local_rows = latents.shape[0]
    block_rows = local_rows // SUB
    gathered = lax.all_gather(latents, "ctx", axis=0, tiled=True)
    key_pos = prompt_positions(
        group_order, jnp.arange(gathered.shape[0], dtype=jnp.int32), block_rows
    )
    own_rows = lax.axis_index("ctx") * local_rows + jnp.arange(local_rows, dtype=jnp.int32)
    query_pos = prompt_positions(group_order, own_rows, block_rows)
    outputs = attend_head(queries, gathered, query_pos, key_pos)
    return outputs


def expert_part(hidden_b, expert_ids, gate_fixed, w_gate, w_up, w_down):
    tok_rows, picks = expert_ids.shape
    width_local = hidden_b.shape[1]
    hidden_ff = w_gate.shape[2]
    experts_n = lax.axis_size("exp")
    capacity = min(tok_rows, max(2, 2 * tok_rows * picks // experts_n))
    all_slots = experts_n * capacity
    flat_ids = expert_ids.reshape(-1)
    choose = (flat_ids[:, None] == jnp.arange(experts_n, dtype=jnp.int32)[None, :]).astype(
        jnp.int32
    )
    before = jnp.cumsum(choose, axis=0) - choose
    slot_of = jnp.sum(before * choose, axis=1)
    target = flat_ids * capacity + slot_of
    place_map = (target[:, None] == jnp.arange(all_slots, dtype=jnp.int32)[None, :]).astype(
        jnp.float32
    )
    pair_token = jnp.arange(tok_rows * picks, dtype=jnp.int32) // picks
    owner_map = (pair_token[:, None] == jnp.arange(tok_rows, dtype=jnp.int32)[None, :]).astype(
        jnp.float32
    )
    route_map = jnp.dot(place_map.T, owner_map, precision=lax.Precision.HIGHEST)
    outgoing = jnp.dot(
        route_map.astype(jnp.bfloat16), hidden_b, preferred_element_type=jnp.float32
    ).astype(jnp.bfloat16)
    incoming = lax.all_to_all(
        outgoing.reshape(experts_n, capacity, width_local),
        "exp",
        split_axis=0,
        concat_axis=0,
        tiled=True,
    )
    received = incoming.reshape(all_slots, width_local)
    gate_w = w_gate[0]
    up_w = w_up[0]
    down_w = w_down[0]
    gate_part = jnp.dot(received, gate_w, preferred_element_type=jnp.float32)
    up_part = jnp.dot(received, up_w, preferred_element_type=jnp.float32)
    summed = lax.psum_scatter(
        jnp.concatenate([gate_part, up_part], axis=1), "ctx", scatter_dimension=0, tiled=True
    )
    inner_act = (jax.nn.silu(summed[:, :hidden_ff]) * summed[:, hidden_ff:]).astype(jnp.bfloat16)
    results = jnp.dot(
        lax.all_gather(inner_act, "ctx", axis=0, tiled=True),
        down_w,
        preferred_element_type=jnp.float32,
    ).astype(jnp.bfloat16)
    returned = lax.all_to_all(
        results.reshape(experts_n, capacity, width_local),
        "exp",
        split_axis=0,
        concat_axis=0,
        tiled=True,
    )
    weights = (gate_fixed.astype(jnp.float32) / 32768.0).reshape(-1)
    mixing = jnp.dot(owner_map.T * weights[None, :], place_map, precision=lax.Precision.HIGHEST)
    combined = jnp.dot(
        mixing,
        returned.reshape(all_slots, width_local).astype(jnp.float32),
        precision=lax.Precision.HIGHEST,
    )
    return combined.astype(jnp.bfloat16)


def per_device(
    queries, latents, group_order, hidden_b, expert_ids, gate_fixed, w_gate, w_up, w_down
):
    attn_out = attention_part(queries, latents, group_order)
    moe_out = expert_part(hidden_b, expert_ids, gate_fixed, w_gate, w_up, w_down)
    return (attn_out, moe_out)


def solution(mesh):
    in_specs = (
        P("ctx", "exp"),
        P("ctx", None),
        P(),
        P("exp", "ctx"),
        P("exp", None),
        P("exp", None),
        P("exp", "ctx", None),
        P("exp", "ctx", None),
        P("exp", None, "ctx"),
    )
    out_specs = (P("ctx", "exp"), P("exp", "ctx"))
    return jax.shard_map(
        per_device, mesh=mesh, in_specs=in_specs, out_specs=out_specs, check_vma=False
    )
```

profile of v0, /device:TPU:6, one launch (start us, length us, event | category | flops | bytes accessed | tf_op | source)
XLA Modules:
  0.0 210.0 jit_solution(6716124397644506324)
XLA Ops:
  7.2 0.9 reshape.107
  8.3 0.2 select_reduce_fusion.1
  8.5 0.3 convolution_convert_fusion.3
  8.7 0.9 convolution_convert_fusion.1
  9.9 33.1 %all_to_all.10 = bf16[64,2,448]{2,1,0:T(2,128)(2,1)S(1)} all-to-all(bf16[64,2,448]{2,1,0:T(2,128)(2,1)S(1)} %reshape.108), channel_id=1, replica_groups=mesh['ctx'=16,'exp'=64] {'exp'}, dimensions={0} | all-to-all | bytes 229376 | tf_op jit(solution)/shard_map/all_to_all | solution.py:74
  43.2 0.3 fusion.8
  43.5 0.3 fusion.10
  43.8 1.0 pad_maximum_fusion
  44.9 0.7 all-gather.2.cloned.1.call-update
  45.9 0.2 fusion.15
  46.1 69.7 %reduce-scatter.2.cloned.1.call-done = f32[8,2048]{1,0:T(8,128)} async-done(((f32[128,2048]{1,0:T(8,128)}), f32[8,2048]{1,0:T(8,128)}) %reduce-scatter.2.cloned.1.call-update) | async-done | bytes 65552 | tf_op jit(solution)/shard_map/reduce_scatter | solution.py:87
  115.8 0.8 fusion.14
  116.6 32.3 %all_gather.7 = bf16[128,1024]{1,0:T(8,128)(2,1)S(1)} all-gather(bf16[8,1024]{1,0:T(8,128)(2,1)S(1)} %fusion.14), channel_id=1, replica_groups=mesh['ctx'=16,'exp'=64] {'ctx'}, dimensions={0}, use_global_device_ids=true | all-gather | bytes 278528 | tf_op jit(solution)/shard_map/all_gather | solution.py:92
  148.9 0.4 convolution_convert_fusion
  149.3 0.1 copy.14
  149.4 0.7 reshape.110
  150.1 14.1 %all-to-all-start.1 = ((bf16[64,2,448]{2,1,0:T(2,128)(2,1)}), bf16[64,2,448]{2,1,0:T(2,128)(2,1)S(1)}, u32[]{:S(2)}, u32[]{:S(2)}) async-start(bf16[64,2,448]{2,1,0:T(2,128)(2,1)} %reshape.110), calls=%async_computation.2 | async-start | bytes 262144 | tf_op jit(solution)/shard_map/all_to_all | solution.py:96
  164.3 0.2 select_reduce_fusion
  164.4 11.2 %all-to-all-done.1 = bf16[64,2,448]{2,1,0:T(2,128)(2,1)S(1)} async-done(((bf16[64,2,448]{2,1,0:T(2,128)(2,1)}), bf16[64,2,448]{2,1,0:T(2,128)(2,1)S(1)}, u32[]{:S(2)}, u32[]{:S(2)}) %all-to-all-start.1) | async-done | bytes 114720 | tf_op jit(solution)/shard_map/all_to_all | solution.py:96
  175.8 0.8 convolution_convert_fusion.2
  176.6 22.3 %all-gather.2.cloned.1.call-done = bf16[2048,576]{0,1:T(8,128)(2,1)} async-done(((bf16[128,576]{0,1:T(8,128)(2,1)}), bf16[2048,576]{0,1:T(8,128)(2,1)}) %all-gather.2.cloned.1.call-update) | async-done | bytes 2359312 | tf_op jit(solution)/shard_map/all_gather | solution.py:39
  198.9 2.5 %fusion.34 = (f32[128]{0:T(128)S(1)}, f32[128,2048]{1,0:T(8,128)S(1)}) fusion(bf16[128,576]{0,1:T(8,128)(2,1)S(1)} %copy-done.4, bf16[2048,576]{0,1:T(8,128)(2,1)} %all-gather.2.cloned.1.call-done, s32[128]{0:T(128)S(1)} %fusion.32, s32[2048]{0:T(1024)S(1)} %fusion.26), kind=kOutput, calls=%fused_computation.66 | convolution fusion | flops 303038336 | bytes 3564544 | tf_op jit(solution)/shard_map/dot_general | solution.py:24
  201.4 0.3 fusion.6
  201.7 1.5 fusion.3
  (31 shorter events, 0.9 us)
Async XLA Ops:
  7.2 36.0 %copy-start = (bf16[1,448,1024]{2,1,0:T(8,128)(2,1)S(1)}, bf16[1,448,1024]{2,1,0:T(8,128)(2,1)}, u32[]{:S(2)}) copy-start(bf16[1,448,1024]{2,1,0:T(8,128)(2,1)} %param.16) | copy-start | bytes 2752516
  7.2 36.3 %copy-start.3 = (bf16[1,448,1024]{2,1,0:T(8,128)(2,1)S(1)}, bf16[1,448,1024]{2,1,0:T(8,128)(2,1)}, u32[]{:S(2)}) copy-start(bf16[1,448,1024]{2,1,0:T(8,128)(2,1)} %param.15) | copy-start | bytes 2752516
  7.2 108.6 %reduce-scatter.2.cloned.1.call-start = ((), (), s32[]{:S(2)}) async-start(), calls=%async_computation.4 | async-start | bytes 1114112 | tf_op jit(solution)/shard_map/reduce_scatter | solution.py:87
  43.5 2.2 %copy-start.5 = (s32[8,8]{1,0:T(8,128)S(1)}, s32[8,8]{1,0:T(8,128)}, u32[]{:S(2)}) copy-start(s32[8,8]{1,0:T(8,128)} %param.14) | copy-start | bytes 772
  43.5 2.3 %copy-start.6 = (s32[64]{0:T(128)S(1)}, s32[64]{0:T(128)}, u32[]{:S(2)}) copy-start(s32[64]{0:T(128)} %param.11) | copy-start | bytes 772
  43.5 105.4 %copy-start.2 = (bf16[1,1024,448]{1,2,0:T(8,128)(2,1)S(1)}, bf16[1,1024,448]{1,2,0:T(8,128)(2,1)}, u32[]{:S(2)}) copy-start(bf16[1,1024,448]{1,2,0:T(8,128)(2,1)} %param.17) | copy-start | bytes 2752516
  44.9 154.0 %copy-start.4 = (bf16[128,576]{0,1:T(8,128)(2,1)S(1)}, bf16[128,576]{0,1:T(8,128)(2,1)}, u32[]{:S(2)}) copy-start(bf16[128,576]{0,1:T(8,128)(2,1)} %param.9) | copy-start | bytes 442372
  44.9 154.0 %all-gather.2.cloned.1.call-start = ((), (), s32[]{:S(2)}) async-start(), calls=%async_computation.3 | async-start | bytes 2506752 | tf_op jit(solution)/shard_map/all_gather | solution.py:39
  150.1 25.5 %all-to-all-start.1 = ((bf16[64,2,448]{2,1,0:T(2,128)(2,1)}), bf16[64,2,448]{2,1,0:T(2,128)(2,1)S(1)}, u32[]{:S(2)}, u32[]{:S(2)}) async-start(bf16[64,2,448]{2,1,0:T(2,128)(2,1)} %reshape.110), calls=%async_computation.2 | async-start | bytes 262144 | tf_op jit(solution)/shard_map/all_to_all | solution.py:96
  198.9 2.8 %copy-start.1 = (bf16[2048,576]{0,1:T(8,128)(2,1)S(1)}, bf16[2048,576]{0,1:T(8,128)(2,1)}, u32[]{:S(2)}) copy-start(bf16[2048,576]{0,1:T(8,128)(2,1)} %all-gather.2.cloned.1.call-done) | copy-start | bytes 7077892
Sparse Core Ops, SparseCore 0:
  45.0 70.7 reduce-scatter.1
  118.7 80.1 all-gather.1
where the time goes:
time: 210 us
  waiting for transfers between devices  104 us (50%)
  blocking collectives  65.5 us (31%)
  starting transfers between devices  14.2 us (7%)
  between operations  14.2 us (7%)
  matrix products  7.18 us (3%)
  other arithmetic  2.79 us (1%)
  local copies, waits for them, and re-layouts  2.24 us (1%)
    reduce_scatter x1, waiting for transfers between devices, expert_part(): lax.psum_scatter(jnp.concatenate([gate_part, up_part], axis=1), 'ctx', sc...  69.7 us
    all_to_all x1, blocking collectives, expert_part(): lax.all_to_all(outgoing.reshape(experts_n, capacity, width_local), 'exp',...  33.1 us
    all_gather x1, blocking collectives, expert_part(): lax.all_gather(inner_act, 'ctx', axis=0, tiled=True)  32.3 us
    all_gather x1, waiting for transfers between devices, attention_part(): gathered = lax.all_gather(latents, 'ctx', axis=0, tiled=True)  22.3 us
    all_to_all x1, starting transfers between devices, expert_part(): lax.all_to_all(results.reshape(experts_n, capacity, width_local), 'exp',...  14.1 us
    all_to_all x1, waiting for transfers between devices, expert_part(): lax.all_to_all(results.reshape(experts_n, capacity, width_local), 'exp',...  11.2 us
  transfers between devices with their start and end apart: 3, of which 3 were waited for; matrix products, arithmetic and copies ran while one was open for 2% of the time, Pallas kernels for 0%

commit v1 on v0

v1 whole, which is shorter than its diff:
```python
import functools
import math

import jax
import jax.numpy as jnp
from jax import lax
from jax.experimental import pallas as pl
from jax.experimental.pallas import tpu as pltpu
from jax.sharding import PartitionSpec as P

MESH = pl.DeviceIdType.MESH
SCALE = 1.0 / math.sqrt(192.0)
KV_RANK = 512
BF = jnp.bfloat16
F32 = jnp.float32
I32 = jnp.int32


def iota(shape, dim):
    return lax.broadcasted_iota(I32, shape, dim)


def dot(a, b, dims=((1,), (0,))):
    return lax.dot_general(a, b, (dims, ((), ())), preferred_element_type=F32)


def kernel(
    q_hbm, lat_hbm, go_ref, hid_ref, ids_ref, gate_ref, wg_hbm, wu_hbm, wd_hbm,
    attn_ref, moe_ref,
    q, lat, wg, wu, wd, pay, hall, part, xin, yin, inner, zbuf, ret, back, comb_hi, comb_lo, scores,
    wsem, qsem, lsem, hx_s, hx_r, hz_s, hz_r, hc_s, hc_r,
    rx_s, rx_r, ry_s, ry_r, ay_s, ay_r, ax_s, ax_r, rt_s, rt_r,
    ly_s, ly_r, lx_s, lx_r, lc_s, lc_r,
):
    c = lax.axis_index("ctx")
    e = lax.axis_index("exp")
    xl, y = c // 8, c % 8
    xh, z, core = e // 16, (e // 2) % 8, e % 2

    def dev(c_, e_):
        return {"ctx": c_, "exp": e_}

    def exp_at(xh_, z_, core_):
        return (xh_ * 8 + z_) * 2 + core_

    def x_peer(k):
        return dev(c, exp_at((xh + k) % 4, z, core))

    def z_peer(k):
        return dev(c, exp_at(xh, (z + k) % 8, core))

    def y_peer(k):
        return dev(xl * 8 + (y + k) % 8, e)

    sibling = dev(c, exp_at(xh, z, 1 - core))
    pair = dev((c + 8) % 16, e)
    far_pair = dev((c + 8) % 16, exp_at((xh + 3 + 2 * xl) % 4, z, core))

    def send(src, dst, ss, rs, to):
        pltpu.make_async_remote_copy(
            src_ref=src, dst_ref=dst, send_sem=ss, recv_sem=rs, device_id=to, device_id_type=MESH
        ).start()

    def wait(like, sem):
        pltpu.make_async_copy(like, like, sem).wait()

    barrier = pltpu.get_barrier_semaphore()

    def hello(to):
        pl.semaphore_signal(barrier, inc=1, device_id=to, device_id_type=MESH)

    @pl.loop(1, 8)
    def _(k):
        hello(z_peer(k))

    @pl.loop(1, 4)
    def _(k):
        hello(x_peer(k))

    @pl.loop(1, 8)
    def _(k):
        hello(y_peer(k))

    hello(sibling)
    hello(pair)
    hello(far_pair)

    half = pl.ds(pl.multiple_of(core * 64, 64), 64)
    lat_copy = pltpu.make_async_copy(lat_hbm.at[half], lat.at[c, half], lsem)
    lat_copy.start()
    w_copies = [
        pltpu.make_async_copy(wg_hbm.at[0], wg.at[pl.ds(0, 448)], wsem.at[0]),
        pltpu.make_async_copy(wu_hbm.at[0], wu.at[pl.ds(0, 448)], wsem.at[1]),
        pltpu.make_async_copy(wd_hbm.at[0], wd, wsem.at[2]),
    ]
    for cp in w_copies:
        cp.start()
    q_copy = pltpu.make_async_copy(q_hbm, q, qsem)
    q_copy.start()

    ids = ids_ref[...].astype(F32)
    pay[...] = jnp.zeros((8, 512), F32)
    pay[:, :448] = hid_ref[...].astype(F32)
    spread = (iota((8, 128), 1) == iota((8, 128), 0) + 64).astype(BF)
    pay[:, 384:] = pay[:, 384:] + dot(ids.astype(BF), spread)
    hall[core, z, xh] = jnp.concatenate([pay[:, :256], pay[:, 256:]], axis=0).astype(BF)
    for w in (wg, wu):
        w[448:, :] = jnp.zeros((64, 1024), BF)
    zbuf[:, 384:] = jnp.zeros((128, 128), F32)

    lat_copy.wait()
    pl.semaphore_wait(barrier, 20)

    @pl.loop(1, 4)
    def _(k):
        mine = hall.at[core, z, xh]
        send(mine, mine, hx_s, hx_r, x_peer(k))

    @pl.loop(1, 8)
    def _(k):
        mine = lat.at[c, half]
        send(mine, mine, ly_s, ly_r, y_peer(k))

    wait(hall.at[0, 0, pl.ds(0, 3)], hx_r)

    @pl.loop(1, 8)
    def _(k):
        mine = hall.at[core, z]
        send(mine, mine, hz_s, hz_r.at[k], z_peer(k))

    send(hall.at[core, z], hall.at[core, z], hc_s, hc_r, sibling)

    @pl.loop(0, 7)
    def _(n):
        k = (n // 2 + 1) * (1 - 2 * (n % 2)) + 8 * (n % 2)
        from_z = hall.at[core, (z + 8 - k) % 8]
        wait(from_z, hz_r.at[k])
        send(from_z, from_z, hc_s, hc_r, sibling)

    wait(hall.at[1 - core], hc_r)

    rows2d = hall[...].reshape(1024, 256)
    id_lane = iota((1024, 128), 1)
    named = jnp.where(
        (rows2d[:, 128:].astype(F32) == e.astype(F32)) & (id_lane >= 64) & (id_lane < 72), 1.0, 0.0
    ).astype(BF)
    hit = dot(jnp.ones((8, 128), BF), named, ((1,), (1,)))
    col = iota((8, 1024), 1)
    tok = col % 8
    hit = jnp.where((col // 8) % 2 == 1, hit, 0.0)
    upto = hit
    for step in (1, 2, 4):
        upto = upto + jnp.where(tok >= step, pltpu.roll(upto, step, 1), 0.0)
    code = jnp.where(hit > 0.5, (col // 16).astype(F32) * 2.0 + upto - hit, -1.0)
    row_id = iota((128, 1024), 0).astype(F32)
    pick_hi = jnp.where(code[:1] == row_id, 1.0, 0.0).astype(BF)
    pick_lo = jnp.where(pltpu.roll(code, 1024 - 8, 1)[:1] == row_id, 1.0, 0.0).astype(BF)
    x_lo = dot(pick_lo, rows2d).astype(BF)
    x_hi = dot(pick_hi, rows2d).astype(BF)

    w_copies[0].wait()
    w_copies[1].wait()
    gate_part = dot(x_lo, wg[:256, :]) + dot(x_hi, wg[256:, :])
    up_part = dot(x_lo, wu[:256, :]) + dot(x_hi, wu[256:, :])
    part[...] = jnp.concatenate(
        [gate_part.reshape(16, 8, 1024), up_part.reshape(16, 8, 1024)], axis=1
    ).astype(BF)

    def far_first(n):
        return 4 + (1 - 2 * (n % 2)) * ((n + 1) // 2)

    other = (1 - xl) * 8

    @pl.loop(0, 8)
    def _(n):
        send(part.at[other + (y + far_first(n)) % 8], xin.at[n], rx_s, rx_r.at[n], pair)

    own_half = lat.at[pl.ds(xl * 8, 8), half]
    wait(lat.at[pl.ds(0, 7), pl.ds(0, 64)], ly_r)
    send(own_half, own_half, lx_s, lx_r, far_pair)
    send(own_half, own_half, lc_s.at[0], lc_r.at[0], sibling)

    def add_pair(n):
        own = xl * 8 + (y + far_first(n)) % 8
        wait(xin.at[n], rx_r.at[n])
        return own, (part[own].astype(F32) + xin[n].astype(F32)).astype(BF)

    @pl.loop(0, 7)
    def _(n):
        own, total = add_pair(n)
        part[own] = total
        send(part.at[own], yin.at[y], ry_s, ry_r, y_peer(far_first(n)))

    _, own_total = add_pair(7)
    yin[y] = own_total
    wait(yin.at[pl.ds(0, 7)], ry_r)
    summed = jnp.sum(yin[...].astype(F32), axis=0)
    gate_sum, up_sum = summed[:8], summed[8:]
    act = gate_sum / (1.0 + jnp.exp(-gate_sum)) * up_sum
    inner[c] = jnp.concatenate([act[:, :512], act[:, 512:]], axis=0).astype(BF)

    @pl.loop(0, 7)
    def _(n):
        k = far_first(n)
        send(inner.at[c], inner.at[c], ay_s, ay_r.at[k], y_peer(k))

    send(inner.at[c], inner.at[c], ax_s, ax_r, pair)

    @pl.loop(0, 7)
    def _(n):
        k = (n // 2 + 1) * (1 - 2 * (n % 2)) + 8 * (n % 2)
        got = inner.at[xl * 8 + (y + 8 - k) % 8]
        wait(got, ay_r.at[k])
        send(got, got, ax_s, ax_r, pair)

    wait(inner.at[pl.ds(0, 8)], ax_r)
    acts = inner[...].astype(F32)
    w_copies[2].wait()
    zbuf[:, :448] = dot(acts[:, :8].reshape(128, 512).astype(BF), wd[:512, :]) + dot(
        acts[:, 8:].reshape(128, 512).astype(BF), wd[512:, :]
    )
    out_row = iota((512, 128), 0)
    in_row = iota((512, 128), 1)
    packed = jnp.zeros((512, 128), F32)
    for j in range(4):
        place = jnp.where(out_row == 4 * in_row + j, 1.0, 0.0).astype(BF)
        packed = packed + dot(place, zbuf[:, 128 * j : 128 * (j + 1)].astype(BF))
    ret[...] = packed.reshape(64, 8, 128).astype(BF)

    me = (core * 8 + z) * 4 + xh

    @pl.loop(1, 64)
    def _(k):
        g = (me + k) % 64
        to = dev(c, exp_at(g % 4, (g // 4) % 8, g // 32))
        send(ret.at[g], back.at[me], rt_s, rt_r, to)

    back[me] = ret[me]

    wait(own_half, lx_r)
    other_half = lat.at[pl.ds(other, 8), half]
    send(other_half, other_half, lc_s.at[1], lc_r.at[1], sibling)

    r_id = iota((512, 32), 0)
    q_id = iota((512, 32), 1)
    grp = r_id // 8
    expert_of_row = (((grp % 4) * 8 + (grp // 4) % 8) * 2 + grp // 32).astype(F32)
    diag = iota((8, 32), 0) == iota((8, 32), 1) % 8
    gates = gate_ref[...].astype(F32)
    found = jnp.zeros((512, 32), F32)
    gated = jnp.zeros((512, 32), F32)
    for k in range(8):
        id_row = jnp.sum(jnp.where(diag, ids[:, k : k + 1], 0.0), axis=0, keepdims=True)
        gate_row = jnp.sum(jnp.where(diag, gates[:, k : k + 1], 0.0), axis=0, keepdims=True)
        same = expert_of_row == id_row
        found = found + jnp.where(same, 1.0, 0.0)
        gated = gated + jnp.where(same, gate_row, 0.0)
    a_id, b_id = iota((32, 32), 0), iota((32, 32), 1)
    earlier = jnp.where((a_id // 8 == b_id // 8) & (a_id < b_id), 1.0, 0.0).astype(BF)
    before = dot(found.astype(BF), earlier)
    mine = (
        (found > 0.5) & (before == ((r_id // 4) % 2).astype(F32)) & (r_id % 4 == q_id // 8)
    )
    weight = jnp.where(mine, gated * (1.0 / 32768.0), 0.0)
    weight_hi = weight.astype(BF)
    comb_hi[...] = weight_hi
    comb_lo[...] = (weight - weight_hi.astype(F32)).astype(BF)

    go = go_ref[...].astype(F32)
    blk = iota((128, 64), 1)
    own_blk = c * 4 + iota((128, 64), 0) // 32
    query_pos = jnp.sum(jnp.where(blk == own_blk, go, 0.0), axis=1, keepdims=True) * 32.0 + (
        iota((128, 1), 0) % 32
    ).astype(F32)
    wait(own_half, lc_r.at[0])
    wait(own_half, lc_r.at[1])
    q_copy.wait()
    queries = q[...]

    def score(i, top):
        keys = lat[pl.ds(i * 2, 2)].reshape(256, 576)
        lane = iota((64, 256), 1)
        owner = jnp.where(iota((64, 256), 0) == i * 8 + lane // 32, 1.0, 0.0).astype(BF)
        base = dot(go.astype(BF), owner)
        key_pos = base * 32.0 + (iota((1, 256), 1) % 32).astype(F32)
        s = dot(queries, keys, ((1,), (1,))) * SCALE
        s = jnp.where(key_pos <= query_pos, s, -1e30)
        scores[i] = s
        return jnp.maximum(top, jnp.max(s, axis=1, keepdims=True))

    top = lax.fori_loop(0, 8, score, jnp.full((128, 1), -1e30, F32))

    def mix(i, carry):
        total, acc = carry
        p = jnp.exp(scores[i] - top)
        values = lat[pl.ds(i * 2, 2), :, :KV_RANK].reshape(256, KV_RANK)
        return total + jnp.sum(p, axis=1, keepdims=True), acc + dot(p.astype(BF), values)

    total, acc = lax.fori_loop(
        0, 8, mix, (jnp.zeros((128, 1), F32), jnp.zeros((128, KV_RANK), F32))
    )
    attn_ref[...] = (acc / total).astype(BF)

    wait(back.at[pl.ds(0, 63)], rt_r)
    rows = back[...].astype(F32).reshape(512, 128).astype(BF)
    mixed = dot(comb_hi[...], rows, ((0,), (0,))) + dot(comb_lo[...], rows, ((0,), (0,)))
    for j in range(4):
        width = min(128, 448 - 128 * j)
        moe_ref[:, 128 * j : 128 * j + width] = mixed[8 * j : 8 * j + 8, :width].astype(BF)

    wait(hall.at[0, 0, pl.ds(0, 3)], hx_s)
    wait(hall.at[0, pl.ds(0, 7)], hz_s)
    wait(hall.at[0], hc_s)
    wait(part.at[pl.ds(0, 8)], rx_s)
    wait(part.at[pl.ds(0, 7)], ry_s)
    wait(inner.at[pl.ds(0, 7)], ay_s)
    wait(inner.at[pl.ds(0, 8)], ax_s)
    wait(ret.at[pl.ds(0, 63)], rt_s)
    wait(lat.at[pl.ds(0, 7), pl.ds(0, 64)], ly_s)
    wait(own_half, lx_s)
    wait(own_half, lc_s.at[0])
    wait(own_half, lc_s.at[1])


def per_device(queries, latents, group_order, hidden_b, expert_ids, gate_fixed, w_gate, w_up, w_down):
    hbm = pl.BlockSpec(memory_space=pl.ANY)
    vmem = pl.BlockSpec(memory_space=pltpu.VMEM)
    dma = pltpu.SemaphoreType.DMA
    return pl.pallas_call(
        kernel,
        out_shape=(
            jax.ShapeDtypeStruct((128, 512), BF),
            jax.ShapeDtypeStruct((8, 448), BF),
        ),
        in_specs=[hbm, hbm, vmem, vmem, vmem, vmem, hbm, hbm, hbm],
        out_specs=(vmem, vmem),
        scratch_shapes=[
            pltpu.VMEM((128, 576), BF),
            pltpu.VMEM((16, 128, 576), BF),
            pltpu.VMEM((512, 1024), BF),
            pltpu.VMEM((512, 1024), BF),
            pltpu.VMEM((1024, 448), BF),
            pltpu.VMEM((8, 512), F32),
            pltpu.VMEM((2, 8, 4, 16, 256), BF),
            pltpu.VMEM((16, 16, 1024), BF),
            pltpu.VMEM((8, 16, 1024), BF),
            pltpu.VMEM((8, 16, 1024), BF),
            pltpu.VMEM((16, 16, 512), BF),
            pltpu.VMEM((128, 512), F32),
            pltpu.VMEM((64, 8, 128), BF),
            pltpu.VMEM((64, 8, 128), BF),
            pltpu.VMEM((512, 32), BF),
            pltpu.VMEM((512, 32), BF),
            pltpu.VMEM((8, 128, 256), F32),
            dma((3,)), dma, dma,
            dma, dma, dma, dma((8,)), dma, dma,
            dma, dma((8,)), dma, dma,
            dma, dma((8,)), dma, dma,
            dma, dma,
            dma, dma, dma, dma, dma((2,)), dma((2,)),
        ],
        compiler_params=pltpu.CompilerParams(
            collective_id=0, has_side_effects=True, vmem_limit_bytes=32 << 20
        ),
        name="layer",
    )(
        queries, latents, group_order.reshape(1, 64), hidden_b, expert_ids, gate_fixed,
        w_gate, w_up, w_down,
    )


def solution(mesh):
    in_specs = (
        P("ctx", "exp"),
        P("ctx", None),
        P(),
        P("exp", "ctx"),
        P("exp", None),
        P("exp", None),
        P("exp", "ctx", None),
        P("exp", "ctx", None),
        P("exp", None, "ctx"),
    )
    out_specs = (P("ctx", "exp"), P("exp", "ctx"))
    return jax.shard_map(
        per_device, mesh=mesh, in_specs=in_specs, out_specs=out_specs, check_vma=False
    )
```

time: 210 us -> 72.2 us (0.34)
  the two profiles are of different devices: /device:TPU:6 before, /device:TPU:1 now
where the time goes in v1:
time: 72.2 us; the launch traced here: 72 us
  Pallas kernels  67 us (93%)
  local copies, waits for them, and re-layouts  4.2 us (6%)
    pallas_call x1, Pallas kernels, per_device(): pl.pallas_call(kernel, out_shape=(jax.ShapeDtypeStruct((128, 512), BF), j...  67 us
    unnamed x19, local copies, waits for them, and re-layouts  4.2 us

profile of v1, /device:TPU:1, one launch (start us, length us, event | category | flops | bytes accessed | tf_op | source)
XLA Modules:
  0.0 72.0 jit_solution(4278509839574161229)
XLA Ops:
  0.6 0.0 copy-start.6
  0.6 1.1 %copy.11.q_hbm = bf16[128,576]{1,0:T(8,128)(2,1)S(1)} copy(bf16[128,576]{0,1:T(8,128)(2,1)} %param.9) | data formatting | bytes 294912 | tf_op args[0]
  1.7 0.0 copy-done.6
  1.7 0.2 copy.12.lat_hbm
  1.9 0.0 copy-start
  1.9 0.0 copy-start.1
  1.9 0.0 copy-start.2
  1.9 0.0 copy-start.3
  2.0 0.0 copy-start.4
  2.0 0.0 copy-start.5
  2.0 1.6 %copy.13.wd_hbm = bf16[1,1024,448]{2,1,0:T(8,128)(2,1)S(1)} copy(bf16[1,1024,448]{1,2,0:T(8,128)(2,1)} %param.17) | data formatting | bytes 1835008 | tf_op args[8]
  3.6 0.0 copy-done
  3.6 0.1 copy-done.1
  3.6 0.0 copy-done.2
  3.7 0.0 copy-done.3
  3.7 0.0 copy-done.4
  3.7 0.0 copy-done.5
  3.7 67.0 %layer.1 = (bf16[128,512]{1,0:T(8,128)(2,1)S(1)}, bf16[8,448]{1,0:T(8,128)(2,1)S(1)}) custom-call(bf16[128,576]{1,0:T(8,128)(2,1)S(1)} %copy.11.q_hbm, bf16[128,576]{1,0:T(8,128)(2,1)S(1)} %copy.12.lat_hbm, s32[1,64]{1,0:T(1,128)S(1)} %bitcast.1, bf16[8,448]{1,0:T(8,128)(2,1)S(1)} %copy-done.2, s32[8,8]{1,0:T(8,128)S(1)} %copy-done.3, s32[8,8]{1,0:T(8,128)S(1)} %copy-done.4, ...), custom_call_target="tpu_custom_call" | custom-call | tf_op jit(solution)/shard_map/layer/pallas_call | solution.py:329
  70.7 0.7 copy.16
  71.4 0.6 copy.17
Async XLA Ops:
  0.6 1.1 %copy-start.6 = (bf16[128,576]{0,1:T(8,128)(2,1)S(1)}, bf16[128,576]{0,1:T(8,128)(2,1)}, u32[]{:S(2)}) copy-start(bf16[128,576]{0,1:T(8,128)(2,1)} %param.10) | copy-start | bytes 442372
  1.9 1.7 %copy-start = (bf16[1,448,1024]{2,1,0:T(8,128)(2,1)S(1)}, bf16[1,448,1024]{2,1,0:T(8,128)(2,1)}, u32[]{:S(2)}) copy-start(bf16[1,448,1024]{2,1,0:T(8,128)(2,1)} %wg_hbm.1) | copy-start | bytes 2752516
  1.9 1.7 %copy-start.1 = (bf16[1,448,1024]{2,1,0:T(8,128)(2,1)S(1)}, bf16[1,448,1024]{2,1,0:T(8,128)(2,1)}, u32[]{:S(2)}) copy-start(bf16[1,448,1024]{2,1,0:T(8,128)(2,1)} %wu_hbm.1) | copy-start | bytes 2752516
  1.9 1.7 %copy-start.2 = (bf16[8,448]{1,0:T(8,128)(2,1)S(1)}, bf16[8,448]{1,0:T(8,128)(2,1)}, u32[]{:S(2)}) copy-start(bf16[8,448]{1,0:T(8,128)(2,1)} %hid_ref.1) | copy-start | bytes 21508
  1.9 1.7 %copy-start.3 = (s32[8,8]{1,0:T(8,128)S(1)}, s32[8,8]{1,0:T(8,128)}, u32[]{:S(2)}) copy-start(s32[8,8]{1,0:T(8,128)} %ids_ref.1) | copy-start | bytes 772
  2.0 1.7 %copy-start.4 = (s32[8,8]{1,0:T(8,128)S(1)}, s32[8,8]{1,0:T(8,128)}, u32[]{:S(2)}) copy-start(s32[8,8]{1,0:T(8,128)} %gate_ref.1) | copy-start | bytes 772
  2.0 1.7 %copy-start.5 = (s32[64]{0:T(128)S(1)}, s32[64]{0:T(128)}, u32[]{:S(2)}) copy-start(s32[64]{0:T(128)} %param.11) | copy-start | bytes 772

commit v2 on v1

v2 whole, which is shorter than its diff:
```python
import functools
import math

import jax
import jax.numpy as jnp
from jax import lax
from jax.experimental import pallas as pl
from jax.experimental.pallas import tpu as pltpu
from jax.sharding import PartitionSpec as P

MESH = pl.DeviceIdType.MESH
SCALE = 1.0 / math.sqrt(192.0)
KV_RANK = 512
BF = jnp.bfloat16
F32 = jnp.float32
I32 = jnp.int32


def iota(shape, dim):
    return lax.broadcasted_iota(I32, shape, dim)


def dot(a, b, dims=((1,), (0,))):
    return lax.dot_general(a, b, (dims, ((), ())), preferred_element_type=F32)


def kernel(
    q_hbm, lat_hbm, go_hbm, hid_hbm, ids_hbm, gate_hbm, wg_hbm, wu_hbm, wd_hbm,
    attn_ref, moe_ref,
    q, lat, wg, wu, wd, go_v, hid_v, ids_v, gate_v, pay, hall, part, own_part, xin, yin, inner, zbuf, ret, back, comb_hi, comb_lo, scores,
    wsem, qsem, lsem, tsem, near, ready, hx_s, hx_r, hz_s, hz_r, hc_s, hc_r,
    rx_s, rx_r, ry_s, ry_r, ay_s, ay_r, ax_s, ax_r, rt_s, rt_r,
    ly_s, ly_r, lz_s, lz_r, lx_s, lx_r, lc_s, lc_r,
):
    c = lax.axis_index("ctx")
    e = lax.axis_index("exp")
    xl, y = c // 8, c % 8
    xh, z, core = e // 16, (e // 2) % 8, e % 2

    def dev(c_, e_):
        return {"ctx": c_, "exp": e_}

    def exp_at(xh_, z_, core_):
        return (xh_ * 8 + z_) * 2 + core_

    def x_peer(k):
        return dev(c, exp_at((xh + k) % 4, z, core))

    def z_peer(k):
        return dev(c, exp_at(xh, (z + k) % 8, core))

    def y_peer(k):
        return dev(xl * 8 + (y + k) % 8, e)

    shift = jnp.where((c == 0) & (e // 16 == 0) & (core == 0), 1, 0)
    turn = (z + 8 - shift) % 8

    def z_at(t):
        return (t + shift) % 8

    def column(t):
        return dev(c, exp_at(xh, z_at(t), core))

    sibling = dev(c, exp_at(xh, z, 1 - core))
    pair = dev((c + 8) % 16, e)
    far_pair = dev((c + 8) % 16, exp_at((xh + 3 + 2 * xl) % 4, z, core))

    def send(src, dst, ss, rs, to):
        pltpu.make_async_remote_copy(
            src_ref=src, dst_ref=dst, send_sem=ss, recv_sem=rs, device_id=to, device_id_type=MESH
        ).start()

    def wait(like, sem):
        pltpu.make_async_copy(like, like, sem).wait()

    barrier = pltpu.get_barrier_semaphore()

    def hello(to, sem=barrier):
        pl.semaphore_signal(sem, inc=1, device_id=to, device_id_type=MESH)

    for to in (x_peer(1), x_peer(3), sibling, pair, far_pair, y_peer(1), y_peer(7)):
        hello(to)

    @pl.loop(turn + 1, 8)
    def _(t):
        hello(column(t))

    small_copies = [
        pltpu.make_async_copy(src, dst, tsem.at[n])
        for n, (src, dst) in enumerate(
            ((hid_hbm, hid_v), (ids_hbm, ids_v), (gate_hbm, gate_v), (go_hbm, go_v))
        )
    ]
    for cp in small_copies:
        cp.start()
    half = pl.ds(pl.multiple_of(core * 288, 16), 288)
    lat_copy = pltpu.make_async_copy(lat_hbm.at[half], lat.at[c, half], lsem)
    late = z >= 6

    @pl.when(z < 6)
    def _():
        lat_copy.start()

    w_copies = [
        pltpu.make_async_copy(wg_hbm.at[0], wg.at[pl.ds(0, 448)], wsem.at[0]),
        pltpu.make_async_copy(wu_hbm.at[0], wu.at[pl.ds(0, 448)], wsem.at[1]),
        pltpu.make_async_copy(wd_hbm.at[0], wd, wsem.at[2]),
    ]
    for cp in w_copies:
        cp.start()
    q_copy = pltpu.make_async_copy(q_hbm, q, qsem)
    q_copy.start()

    for cp in small_copies:
        cp.wait()
    ids = ids_v[...].astype(F32)
    pay[...] = jnp.zeros((8, 512), F32)
    pay[:, :448] = hid_v[...].astype(F32)
    spread = (iota((8, 128), 1) == iota((8, 128), 0) + 64).astype(BF)
    pay[:, 384:] = pay[:, 384:] + dot(ids.astype(BF), spread)
    hall[core, z, xh] = jnp.concatenate([pay[:, :256], pay[:, 256:]], axis=0).astype(BF)
    for w in (wg, wu):
        w[448:, :] = jnp.zeros((64, 1024), BF)
    zbuf[:, 384:] = jnp.zeros((128, 128), F32)

    pl.semaphore_wait(barrier, 7 + turn)

    @pl.loop(0, turn)
    def _(t):
        hello(column(t), ready.at[turn])

    def greet_y(n):
        hello(y_peer(1), near.at[n, 0])
        hello(y_peer(7), near.at[n, 1])

    def greeted_y(n):
        pl.semaphore_wait(near.at[n, 0], 1)
        pl.semaphore_wait(near.at[n, 1], 1)

    mine = hall.at[core, z, xh]
    send(mine, mine, hx_s, hx_r.at[0], x_peer(1))
    send(mine, mine, hx_s, hx_r.at[1], x_peer(3))
    greet_y(0)
    before_me = hall.at[core, z, (xh + 3) % 4]
    wait(before_me, hx_r.at[0])
    send(before_me, before_me, hx_s, hx_r.at[2], x_peer(1))
    greeted_y(0)
    greet_y(1)
    wait(mine, hx_r.at[1])
    wait(mine, hx_r.at[2])

    slab = hall.at[core, z]

    @pl.loop(0, turn)
    def _(t):
        send(slab, slab, hz_s, hz_r.at[turn], column(t))

    send(slab, slab, hc_s, hc_r, sibling)
    greeted_y(1)
    greet_y(2)

    @pl.when(z < 6)
    def _():
        greeted_y(2)
        lat_copy.wait()

        @pl.loop(1, 8)
        def _(k):
            block = lat.at[c, half]
            send(block, block, ly_s, ly_r, y_peer(k))

    @pl.loop(turn + 1, 8)
    def _(t):
        pl.semaphore_wait(ready.at[t], 1)
        send(slab, slab, hz_s, hz_r.at[turn], column(t))

    @pl.when(late)
    def _():
        greeted_y(2)

    @pl.loop(0, 7)
    def _(n):
        t = jnp.where(n < turn, (n % 2) * (n // 2) + (1 - n % 2) * (turn - 1 - n // 2), n + 1)
        from_z = hall.at[core, z_at(t)]
        wait(from_z, hz_r.at[t])
        send(from_z, from_z, hc_s, hc_r, sibling)

    wait(hall.at[1 - core], hc_r)

    rows2d = hall[...].reshape(1024, 256)
    id_lane = iota((1024, 128), 1)
    named = jnp.where(
        (rows2d[:, 128:].astype(F32) == e.astype(F32)) & (id_lane >= 64) & (id_lane < 72), 1.0, 0.0
    ).astype(BF)
    hit = dot(jnp.ones((8, 128), BF), named, ((1,), (1,)))
    col = iota((8, 1024), 1)
    tok = col % 8
    hit = jnp.where((col // 8) % 2 == 1, hit, 0.0)
    upto = hit
    for step in (1, 2, 4):
        upto = upto + jnp.where(tok >= step, pltpu.roll(upto, step, 1), 0.0)
    code = jnp.where(hit > 0.5, (col // 16).astype(F32) * 2.0 + upto - hit, -1.0)
    row_id = iota((128, 1024), 0).astype(F32)
    pick_hi = jnp.where(code[:1] == row_id, 1.0, 0.0).astype(BF)
    pick_lo = jnp.where(pltpu.roll(code, 1024 - 8, 1)[:1] == row_id, 1.0, 0.0).astype(BF)
    x_lo = dot(pick_lo, rows2d).astype(BF)
    x_hi = dot(pick_hi, rows2d).astype(BF)

    w_copies[0].wait()
    w_copies[1].wait()

    def far_first(n):
        return 4 + (1 - 2 * (n % 2)) * ((n + 1) // 2)

    other = (1 - xl) * 8

    for h in range(2):
        units = slice(512 * h, 512 * (h + 1))
        gate_part = dot(x_lo, wg[:256, units]) + dot(x_hi, wg[256:, units])
        up_part = dot(x_lo, wu[:256, units]) + dot(x_hi, wu[256:, units])
        own_part[h] = jnp.concatenate(
            [gate_part.reshape(16, 8, 512), up_part.reshape(16, 8, 512)], axis=1
        )
        part[h] = own_part[h].astype(BF)

        @pl.loop(0, 8)
        def _(n):
            send(
                part.at[h, other + (y + far_first(n)) % 8], xin.at[h, n],
                rx_s.at[h], rx_r.at[h, n], pair,
            )

    own_half = lat.at[pl.ds(xl * 8, 8), half]
    other_half = lat.at[pl.ds(other, 8), half]

    def latents_along_x():
        send(own_half, own_half, lx_s, lx_r, far_pair)
        send(own_half, own_half, lc_s.at[0], lc_r.at[0], sibling)

    def latents_across():
        wait(own_half, lx_r)
        send(other_half, other_half, lc_s.at[1], lc_r.at[1], sibling)

    @pl.when(z < 6)
    def _():
        wait(lat.at[pl.ds(0, 7), pl.ds(0, 288)], ly_r)
        latents_along_x()

    @pl.when((z == 0) | (z == 5))
    def _():
        to_late = dev(c, exp_at(xh, jnp.where(z == 0, 7, 6), core))
        send(own_half, own_half, lz_s, lz_r, to_late)

    def add_pair(h, n):
        own = xl * 8 + (y + far_first(n)) % 8
        wait(xin.at[h, n], rx_r.at[h, n])
        return own, own_part[h, own] + xin[h, n].astype(F32)

    own_totals = []
    for h in range(2):
        @pl.loop(0, 7)
        def _(n):
            own, total = add_pair(h, n)
            part[h, own] = total.astype(BF)
            send(part.at[h, own], yin.at[h, y], ry_s.at[h], ry_r.at[h], y_peer(far_first(n)))

        own_totals.append(add_pair(h, 7)[1])
        yin[h, y] = jnp.zeros((16, 512), BF)

    for h in range(2):
        wait(yin.at[h, pl.ds(0, 7)], ry_r.at[h])
        summed = own_totals[h] + jnp.sum(yin[h].astype(F32), axis=0)
        gate_sum, up_sum = summed[:8], summed[8:]
        act = gate_sum / (1.0 + jnp.exp(-gate_sum)) * up_sum
        inner[h, c] = jnp.concatenate([act[:, :256], act[:, 256:]], axis=0).astype(BF)
        own_act = inner.at[h, c]

        @pl.loop(0, 8)
        def _(n):
            k = far_first(n)
            send(own_act, own_act, ax_s.at[h], ax_r.at[h], dev(other + (y + k) % 8, e))

            @pl.when(n < 7)
            def _():
                send(own_act, own_act, ay_s.at[h], ay_r.at[h], y_peer(k))

    @pl.when(z < 6)
    def _():
        latents_across()

    @pl.when(late)
    def _():
        wait(own_half, lz_r)
        latents_along_x()

    w_copies[2].wait()
    result = jnp.zeros((128, 448), F32)
    for h in range(2):
        wait(inner.at[h, pl.ds(0, 7)], ay_r.at[h])
        wait(inner.at[h, pl.ds(0, 8)], ax_r.at[h])
        acts = inner[h].astype(F32)
        for u, rows in enumerate((acts[:, :8], acts[:, 8:])):
            first = 512 * h + 256 * u
            result = result + dot(
                rows.reshape(128, 256).astype(BF), wd[:, first : first + 256], ((1,), (1,))
            )
    zbuf[:, :448] = result
    out_row = iota((512, 128), 0)
    in_row = iota((512, 128), 1)
    packed = jnp.zeros((512, 128), F32)
    for j in range(4):
        place = jnp.where(out_row == 4 * in_row + j, 1.0, 0.0).astype(BF)
        packed = packed + dot(place, zbuf[:, 128 * j : 128 * (j + 1)].astype(BF))
    ret[...] = packed.reshape(64, 8, 128).astype(BF)

    me = (core * 8 + z) * 4 + xh

    @pl.loop(0, 63)
    def _(n):
        m = n % 8 // 2
        to_z = (z + far_first(n // 8)) % 8
        to_x = (xh + 2 + (1 - 2 * (m % 2)) * ((m + 1) // 2)) % 4
        to_core = (core + 1 - n % 2) % 2
        g = (to_core * 8 + to_z) * 4 + to_x
        send(ret.at[g], back.at[me], rt_s, rt_r, dev(c, exp_at(to_x, to_z, to_core)))

    back[me] = ret[me]

    @pl.when(late)
    def _():
        latents_across()

    r_id = iota((512, 32), 0)
    q_id = iota((512, 32), 1)
    grp = r_id // 8
    expert_of_row = (((grp % 4) * 8 + (grp // 4) % 8) * 2 + grp // 32).astype(F32)
    diag = iota((8, 32), 0) == iota((8, 32), 1) % 8
    gates = gate_v[...].astype(F32)
    found = jnp.zeros((512, 32), F32)
    gated = jnp.zeros((512, 32), F32)
    for k in range(8):
        id_row = jnp.sum(jnp.where(diag, ids[:, k : k + 1], 0.0), axis=0, keepdims=True)
        gate_row = jnp.sum(jnp.where(diag, gates[:, k : k + 1], 0.0), axis=0, keepdims=True)
        same = expert_of_row == id_row
        found = found + jnp.where(same, 1.0, 0.0)
        gated = gated + jnp.where(same, gate_row, 0.0)
    a_id, b_id = iota((32, 32), 0), iota((32, 32), 1)
    earlier = jnp.where((a_id // 8 == b_id // 8) & (a_id < b_id), 1.0, 0.0).astype(BF)
    before = dot(found.astype(BF), earlier)
    mine = (
        (found > 0.5) & (before == ((r_id // 4) % 2).astype(F32)) & (r_id % 4 == q_id // 8)
    )
    weight = jnp.where(mine, gated * (1.0 / 32768.0), 0.0)
    weight_hi = weight.astype(BF)
    comb_hi[...] = weight_hi
    comb_lo[...] = (weight - weight_hi.astype(F32)).astype(BF)

    go = go_v[...].astype(F32)
    blk = iota((128, 64), 1)
    own_blk = c * 4 + iota((128, 64), 0) // 32
    query_pos = jnp.sum(jnp.where(blk == own_blk, go, 0.0), axis=1, keepdims=True) * 32.0 + (
        iota((128, 1), 0) % 32
    ).astype(F32)
    wait(own_half, lc_r.at[0])
    wait(own_half, lc_r.at[1])
    q_copy.wait()
    eye = jnp.where(iota((128, 128), 0) == iota((128, 128), 1), 1.0, 0.0).astype(BF)
    queries = dot(eye, q[...], ((1,), (1,))).astype(BF)

    def score(i, top):
        keys = jnp.concatenate([lat[2 * i], lat[2 * i + 1]], axis=1)
        lane = iota((64, 256), 1)
        owner = jnp.where(iota((64, 256), 0) == i * 8 + lane // 32, 1.0, 0.0).astype(BF)
        base = dot(go.astype(BF), owner)
        key_pos = base * 32.0 + (iota((1, 256), 1) % 32).astype(F32)
        s = dot(queries, keys) * SCALE
        s = jnp.where(key_pos <= query_pos, s, -1e30)
        scores[i] = s
        return jnp.maximum(top, jnp.max(s, axis=1, keepdims=True))

    top = lax.fori_loop(0, 8, score, jnp.full((128, 1), -1e30, F32))

    def mix(i, carry):
        total, acc = carry
        p = jnp.exp(scores[i] - top)
        values = jnp.concatenate([lat[2 * i, :KV_RANK], lat[2 * i + 1, :KV_RANK]], axis=1)
        return total + jnp.sum(p, axis=1, keepdims=True), acc + dot(p.astype(BF), values, ((1,), (1,)))

    total, acc = lax.fori_loop(
        0, 8, mix, (jnp.zeros((128, 1), F32), jnp.zeros((128, KV_RANK), F32))
    )
    attn_ref[...] = (acc / total).astype(BF)

    wait(back.at[pl.ds(0, 63)], rt_r)
    rows = back[...].astype(F32).reshape(512, 128).astype(BF)
    mixed = dot(comb_hi[...], rows, ((0,), (0,))) + dot(comb_lo[...], rows, ((0,), (0,)))
    for j in range(4):
        width = min(128, 448 - 128 * j)
        moe_ref[:, 128 * j : 128 * j + width] = mixed[8 * j : 8 * j + 8, :width].astype(BF)

    wait(hall.at[0, 0, pl.ds(0, 3)], hx_s)
    wait(hall.at[0, pl.ds(0, 7)], hz_s)
    wait(hall.at[0], hc_s)
    for h in range(2):
        wait(part.at[h, pl.ds(0, 8)], rx_s.at[h])
        wait(part.at[h, pl.ds(0, 7)], ry_s.at[h])
        wait(inner.at[h, pl.ds(0, 7)], ay_s.at[h])
        wait(inner.at[h, pl.ds(0, 8)], ax_s.at[h])
    wait(ret.at[pl.ds(0, 63)], rt_s)
    @pl.when(z < 6)
    def _():
        wait(lat.at[pl.ds(0, 7), pl.ds(0, 288)], ly_s)

    @pl.when((z == 0) | (z == 5))
    def _():
        wait(own_half, lz_s)

    wait(own_half, lx_s)
    wait(own_half, lc_s.at[0])
    wait(own_half, lc_s.at[1])


def per_device(queries, latents, group_order, hidden_b, expert_ids, gate_fixed, w_gate, w_up, w_down):
    hbm = pl.BlockSpec(memory_space=pltpu.HBM)
    vmem = pl.BlockSpec(memory_space=pltpu.VMEM)
    dma = pltpu.SemaphoreType.DMA
    return pl.pallas_call(
        kernel,
        out_shape=(
            pltpu.VMEM((128, 512), BF),
            pltpu.VMEM((8, 448), BF),
        ),
        in_specs=[hbm] * 9,
        out_specs=(vmem, vmem),
        scratch_shapes=[
            pltpu.VMEM((576, 128), BF),
            pltpu.VMEM((16, 576, 128), BF),
            pltpu.VMEM((512, 1024), BF),
            pltpu.VMEM((512, 1024), BF),
            pltpu.VMEM((448, 1024), BF),
            pltpu.VMEM((1, 64), I32),
            pltpu.VMEM((8, 448), BF),
            pltpu.VMEM((8, 8), I32),
            pltpu.VMEM((8, 8), I32),
            pltpu.VMEM((8, 512), F32),
            pltpu.VMEM((2, 8, 4, 16, 256), BF),
            pltpu.VMEM((2, 16, 16, 512), BF),
            pltpu.VMEM((2, 16, 16, 512), F32),
            pltpu.VMEM((2, 8, 16, 512), BF),
            pltpu.VMEM((2, 8, 16, 512), BF),
            pltpu.VMEM((2, 16, 16, 256), BF),
            pltpu.VMEM((128, 512), F32),
            pltpu.VMEM((64, 8, 128), BF),
            pltpu.VMEM((64, 8, 128), BF),
            pltpu.VMEM((512, 32), BF),
            pltpu.VMEM((512, 32), BF),
            pltpu.VMEM((8, 128, 256), F32),
            dma((3,)), dma, dma, dma((4,)),
            pltpu.SemaphoreType.REGULAR((3, 2)),
            pltpu.SemaphoreType.REGULAR((8,)),
            dma, dma((3,)), dma, dma((8,)), dma, dma,
            dma((2,)), dma((2, 8)), dma((2,)), dma((2,)),
            dma((2,)), dma((2,)), dma((2,)), dma((2,)),
            dma, dma,
            dma, dma, dma, dma, dma, dma, dma((2,)), dma((2,)),
        ],
        compiler_params=pltpu.CompilerParams(
            collective_id=0, has_side_effects=True, vmem_limit_bytes=60 << 20
        ),
        name="layer",
    )(
        queries.T, latents.T, group_order.reshape(1, 64), hidden_b, expert_ids, gate_fixed,
        w_gate, w_up, jnp.swapaxes(w_down, 1, 2),
    )


def solution(mesh):
    in_specs = (
        P("ctx", "exp"),
        P("ctx", None),
        P(),
        P("exp", "ctx"),
        P("exp", None),
        P("exp", None),
        P("exp", "ctx", None),
        P("exp", "ctx", None),
        P("exp", None, "ctx"),
    )
    out_specs = (P("ctx", "exp"), P("exp", "ctx"))
    return jax.shard_map(
        per_device, mesh=mesh, in_specs=in_specs, out_specs=out_specs, check_vma=False
    )
```

time: 72.2 us -> 73.4 us (1.017)
  the two profiles are of different devices: /device:TPU:1 before, /device:TPU:52 now
where the time goes in v2:
time: 73.4 us; the launch traced here: 73.2 us
  Pallas kernels  71.3 us (97%)
  local copies, waits for them, and re-layouts  1.26 us (2%)
    pallas_call x1, Pallas kernels, per_device(): pl.pallas_call(kernel, out_shape=(pltpu.VMEM((128, 512), BF), pltpu.VMEM(...  71.3 us

profile of v2, /device:TPU:52, one launch (start us, length us, event | category | flops | bytes accessed | tf_op | source)
XLA Modules:
  0.0 73.2 jit_solution(652387088390582916)
XLA Ops:
  0.6 71.3 %layer.1 = (bf16[128,512]{1,0:T(8,128)(2,1)S(1)}, bf16[8,448]{1,0:T(8,128)(2,1)S(1)}) custom-call(bf16[576,128]{1,0:T(8,128)(2,1)} %bitcast.5, bf16[576,128]{1,0:T(8,128)(2,1)} %bitcast.6, s32[1,64]{1,0:T(1,128)} %bitcast.7, bf16[8,448]{1,0:T(8,128)(2,1)} %hid_hbm.1, s32[8,8]{1,0:T(8,128)} %ids_hbm.1, s32[8,8]{1,0:T(8,128)} %gate_hbm.1, ...), custom_call_target="tpu_custom_call" | custom-call | tf_op jit(solution)/shard_map/layer/pallas_call | solution.py:427
  71.9 0.7 copy.13
  72.6 0.6 copy.14

commit v3 on v2

--- a/solution.py
+++ b/solution.py
@@ -30,7 +30,7 @@
     q, lat, wg, wu, wd, go_v, hid_v, ids_v, gate_v, pay, hall, part, own_part, xin, yin, inner, zbuf, ret, back, comb_hi, comb_lo, scores,
     wsem, qsem, lsem, tsem, near, ready, hx_s, hx_r, hz_s, hz_r, hc_s, hc_r,
     rx_s, rx_r, ry_s, ry_r, ay_s, ay_r, ax_s, ax_r, rt_s, rt_r,
-    ly_s, ly_r, lz_s, lz_r, lx_s, lx_r, lc_s, lc_r,
+    ly_s, ly_r, lx_s, lx_r, lc_s, lc_r,
 ):
     c = lax.axis_index("ctx")
     e = lax.axis_index("exp")
@@ -95,12 +95,7 @@
         cp.start()
     half = pl.ds(pl.multiple_of(core * 288, 16), 288)
     lat_copy = pltpu.make_async_copy(lat_hbm.at[half], lat.at[c, half], lsem)
-    late = z >= 6
-
-    @pl.when(z < 6)
-    def _():
-        lat_copy.start()
-
+    lat_copy.start()
     w_copies = [
         pltpu.make_async_copy(wg_hbm.at[0], wg.at[pl.ds(0, 448)], wsem.at[0]),
         pltpu.make_async_copy(wu_hbm.at[0], wu.at[pl.ds(0, 448)], wsem.at[1]),
@@ -158,25 +153,28 @@
     send(slab, slab, hc_s, hc_r, sibling)
     greeted_y(1)
     greet_y(2)
-
-    @pl.when(z < 6)
-    def _():
+    lat_copy.wait()
+
+    def latents_along_y():
         greeted_y(2)
-        lat_copy.wait()
 
         @pl.loop(1, 8)
         def _(k):
             block = lat.at[c, half]
             send(block, block, ly_s, ly_r, y_peer(k))
 
+    @pl.when(z < 6)
+    def _():
+        latents_along_y()
+
     @pl.loop(turn + 1, 8)
     def _(t):
         pl.semaphore_wait(ready.at[t], 1)
         send(slab, slab, hz_s, hz_r.at[turn], column(t))
 
-    @pl.when(late)
-    def _():
-        greeted_y(2)
+    @pl.when(z >= 6)
+    def _():
+        latents_along_y()
 
     @pl.loop(0, 7)
     def _(n):
@@ -234,6 +232,7 @@
     other_half = lat.at[pl.ds(other, 8), half]
 
     def latents_along_x():
+        wait(lat.at[pl.ds(0, 7), pl.ds(0, 288)], ly_r)
         send(own_half, own_half, lx_s, lx_r, far_pair)
         send(own_half, own_half, lc_s.at[0], lc_r.at[0], sibling)
 
@@ -243,13 +242,7 @@
 
     @pl.when(z < 6)
     def _():
-        wait(lat.at[pl.ds(0, 7), pl.ds(0, 288)], ly_r)
         latents_along_x()
-
-    @pl.when((z == 0) | (z == 5))
-    def _():
-        to_late = dev(c, exp_at(xh, jnp.where(z == 0, 7, 6), core))
-        send(own_half, own_half, lz_s, lz_r, to_late)
 
     def add_pair(h, n):
         own = xl * 8 + (y + far_first(n)) % 8
@@ -267,6 +260,10 @@
         own_totals.append(add_pair(h, 7)[1])
         yin[h, y] = jnp.zeros((16, 512), BF)
 
+    @pl.when(z >= 6)
+    def _():
+        latents_along_x()
+
     for h in range(2):
         wait(yin.at[h, pl.ds(0, 7)], ry_r.at[h])
         summed = own_totals[h] + jnp.sum(yin[h].astype(F32), axis=0)
@@ -287,11 +284,6 @@
     @pl.when(z < 6)
     def _():
         latents_across()
-
-    @pl.when(late)
-    def _():
-        wait(own_half, lz_r)
-        latents_along_x()
 
     w_copies[2].wait()
     result = jnp.zeros((128, 448), F32)
@@ -326,7 +318,7 @@
 
     back[me] = ret[me]
 
-    @pl.when(late)
+    @pl.when(z >= 6)
     def _():
         latents_across()
 
@@ -407,14 +399,7 @@
         wait(inner.at[h, pl.ds(0, 7)], ay_s.at[h])
         wait(inner.at[h, pl.ds(0, 8)], ax_s.at[h])
     wait(ret.at[pl.ds(0, 63)], rt_s)
-    @pl.when(z < 6)
-    def _():
-        wait(lat.at[pl.ds(0, 7), pl.ds(0, 288)], ly_s)
-
-    @pl.when((z == 0) | (z == 5))
-    def _():
-        wait(own_half, lz_s)
-
+    wait(lat.at[pl.ds(0, 7), pl.ds(0, 288)], ly_s)
     wait(own_half, lx_s)
     wait(own_half, lc_s.at[0])
     wait(own_half, lc_s.at[1])
@@ -462,7 +447,7 @@
             dma((2,)), dma((2, 8)), dma((2,)), dma((2,)),
             dma((2,)), dma((2,)), dma((2,)), dma((2,)),
             dma, dma,
-            dma, dma, dma, dma, dma, dma, dma((2,)), dma((2,)),
+            dma, dma, dma, dma, dma((2,)), dma((2,)),
         ],
         compiler_params=pltpu.CompilerParams(
             collective_id=0, has_side_effects=True, vmem_limit_bytes=60 << 20

time: 73.4 us -> 68.7 us (0.936)
  the two profiles are of different devices: /device:TPU:52 before, /device:TPU:1 now
where the time goes in v3:
time: 68.7 us; the launch traced here: 68.6 us
  Pallas kernels  66.7 us (97%)
  local copies, waits for them, and re-layouts  1.26 us (2%)
    pallas_call x1, Pallas kernels, per_device(): pl.pallas_call(kernel, out_shape=(pltpu.VMEM((128, 512), BF), pltpu.VMEM(...  66.7 us

profile of v3, /device:TPU:1, one launch (start us, length us, event | category | flops | bytes accessed | tf_op | source)
XLA Modules:
  0.0 68.6 jit_solution(9141923260702492187)
XLA Ops:
  0.6 66.7 %layer.1 = (bf16[128,512]{1,0:T(8,128)(2,1)S(1)}, bf16[8,448]{1,0:T(8,128)(2,1)S(1)}) custom-call(bf16[576,128]{1,0:T(8,128)(2,1)} %bitcast.5, bf16[576,128]{1,0:T(8,128)(2,1)} %bitcast.6, s32[1,64]{1,0:T(1,128)} %bitcast.7, bf16[8,448]{1,0:T(8,128)(2,1)} %hid_hbm.1, s32[8,8]{1,0:T(8,128)} %ids_hbm.1, s32[8,8]{1,0:T(8,128)} %gate_hbm.1, ...), custom_call_target="tpu_custom_call" | custom-call | tf_op jit(solution)/shard_map/layer/pallas_call | solution.py:412
  67.3 0.7 copy.13
  68.0 0.6 copy.14
